TPU v7x, 32 devices: a whole 2x2x4 slice. The times are simulated.
32 devices in a mesh: groups: 2 (over x), rep: 16 (over z, y, core).
Axes of the slice: x: 2, y: 2, z: 4, core: 2. Of those that a mesh axis runs over, the one named last changes fastest.
Arguments:
- features: float32 [24576, 256], P(('groups', 'rep')), parts along dimension 0, may hold values from -6 to 6
- weight: bfloat16 [256, 256], replicated, may hold values from -0.375 to 0.375
- adjacency: bfloat16 [192, 60, 128, 128], P(('groups', 'rep')), parts along dimension 0, may hold values from -0.0625 to 0.0625
- col_tiles: int32 [192, 60], P(('groups', 'rep')), parts along dimension 0, may hold values from 0 to 95, as said below
Outputs:
- hidden_out: float32 [24576, 256], P(('groups', 'rep')), parts along dimension 0
There are 2 independent parts, one for each index of `groups`. A program takes and returns all parts, laid end to end along the dimension named above; an argument that names none is the same for every part. Nothing has to cross between parts.
Inputs may be any that keep to these rules, and one draw needn't show every extreme that they name: `col_tiles`: the 60 column tiles of one row tile differ. The row tiles of one device, 6 of them, name exactly 4 distinct tiles among the 6 row tiles of every device, its own included.
All inputs are finite; a program needn't handle non-finite values.
Results may differ from a plain program's by a relative error of at most 0.0041.
Values may be sent and summed in bfloat16 or wider, within the bound.
A program may use at most 128 MiB of HBM per device.

v0:
```python
import jax
import jax.numpy as jnp
from jax import lax
from jax.sharding import PartitionSpec as P


def shards(features, weight, adjacency, col_tiles):
    tile_rows = adjacency.shape[2]
    feat_width = features.shape[1]
    projected = jnp.dot(
        features.astype(jnp.bfloat16), weight, preferred_element_type=jnp.float32
    ).astype(jnp.bfloat16)
    everything = lax.all_gather(projected, "rep", axis=0, tiled=True)
    source = everything.reshape(-1, tile_rows, feat_width)
    picked = source[col_tiles]
    summed = jnp.einsum("jkab,jkbf->jaf", adjacency, picked, preferred_element_type=jnp.float32)
    return jnp.maximum(summed, 0.0).reshape(-1, feat_width)


def solution(mesh):
    return jax.shard_map(
        shards,
        mesh=mesh,
        in_specs=(
            P(("groups", "rep"), None),
            P(),
            P(("groups", "rep"), None, None, None),
            P(("groups", "rep"), None),
        ),
        out_specs=P(("groups", "rep"), None),
        check_vma=False,
    )
```

profile of v0, /device:TPU:1, one launch (start us, length us, event | category | flops | bytes accessed | tf_op | source)
XLA Modules:
  0.0 109.8 jit_solution(7598370250300906894)
XLA Ops:
  6.5 0.0 copy-start
  6.5 0.0 all-gather.2.cloned.1.call-start
  6.5 0.9 copy-done
  7.4 2.1 %convolution_convert_fusion = bf16[768,256]{1,0:T(8,128)(2,1)} fusion(bf16[256,256]{1,0:T(8,128)(2,1)S(1)} %copy-done, f32[768,256]{1,0:T(8,128)} %param.4), kind=kOutput, calls=%fused_computation.3 | convolution fusion | flops 101056512 | bytes 1310720 | tf_op jit(solution)/shard_map/dot_general | solution.py:10
  9.6 0.0 all-gather.2.cloned.1.call-update
  9.6 0.7 compare_select_fusion
  10.3 0.1 reshape.10
  10.4 63.7 %all-gather.2.cloned.1.call-done = bf16[12288,256]{1,0:T(8,128)(2,1)} async-done(((bf16[768,256]{1,0:T(8,128)(2,1)}), bf16[12288,256]{1,0:T(8,128)(2,1)}) %all-gather.2.cloned.1.call-update) | async-done | bytes 6291472 | tf_op jit(solution)/shard_map/all_gather | solution.py:13
  74.1 13.8 %gather_fusion = bf16[360,128,256]{2,1,0:T(8,128)(2,1)} fusion(bf16[96,128,256]{2,1,0:T(8,128)(2,1)} %bitcast.14, s32[1024]{0:T(1024)S(1)} %pad_clamp_fusion), kind=kCustom, calls=%fused_computation | custom fusion | bytes 47187360 | tf_op jit(solution)/shard_map/gather | solution.py:15
  87.9 15.0 %fusion = f32[6,256,128]{1,2,0:T(8,128)} fusion(bf16[6,60,128,128]{3,2,1,0:T(8,128)(2,1)} %param.6, bf16[6,60,128,256]{3,2,1,0:T(8,128)(2,1)} %bitcast.13), kind=kOutput, calls=%fused_computation.2 | convolution fusion | flops 3020095488 | bytes 36175872 | tf_op jit(solution)/shard_map/jkab,jkbf->jaf/dot_general | solution.py:16
  (1 shorter events, 0.0 us)
Async XLA Ops:
  6.5 0.9 copy-start
  6.5 67.6 %all-gather.2.cloned.1.call-start = ((), (), s32[]{:S(2)}) async-start(), calls=%async_computation | async-start | bytes 6684672 | tf_op jit(solution)/shard_map/all_gather | solution.py:13
Sparse Core Ops, SparseCore 0:
  9.7 64.3 all-gather.1
where the time goes:
time: 110 us
  waiting for transfers between devices  63.7 us (58%)
  matrix products  17.2 us (16%)
  local copies, waits for them, and re-layouts  14.8 us (13%)
  between operations  13.4 us (12%)
    all_gather x1, waiting for transfers between devices, shards(): everything = lax.all_gather(projected, 'rep', axis=0, tiled=True)  63.7 us
    dot_general x1, matrix products, shards(): jnp.einsum('jkab,jkbf->jaf', adjacency, picked, preferred_element_type=jn...  15 us
    gather x1, local copies, waits for them, and re-layouts, shards(): picked = source[col_tiles]  13.8 us
  transfers between devices with their start and end apart: 1, of which 1 were waited for; matrix products, arithmetic and copies ran while one was open for 1% of the time, Pallas kernels for 0%

commit v1 on v0

v1 whole, which is shorter than its diff:
```python
import functools

import jax
import jax.numpy as jnp
from jax import lax
from jax.experimental import pallas as pl
from jax.experimental.pallas import tpu as pltpu
from jax.sharding import PartitionSpec as P

MESH = pl.DeviceIdType.MESH


def kernel(depth, tiles, feat_ref, weight_ref, slot_ref, adj_ref, out_ref,
           held, adj, adj_sem, recv_sem, z_sem, y_sem, c_sem):
    rep = depth * 4
    every = rep * tiles
    rows = held.shape[1]
    stored = adj_ref.shape[0]
    last = tiles - 1
    me = lax.axis_index("rep")
    c = lax.rem(me, 2)
    y = lax.rem(me // 2, 2)
    z = me // 4
    up, down = me + 4, me - 4
    across, twin = me + 2 - 4 * y, me + 1 - 2 * c
    has_up, has_down = z < depth - 1, z > 0

    def block(zz, yy, cc):
        return (zz * 2 + yy) * 2 + cc

    def copy(tile, sem, target):
        return pltpu.make_async_remote_copy(
            src_ref=held.at[tile], dst_ref=held.at[tile], send_sem=sem,
            recv_sem=recv_sem.at[tile], device_id={"rep": target}, device_id_type=MESH)

    def arrived(tile):
        copy(tile, c_sem.at[0], twin).wait_recv()

    def unit(zz, u):
        if u == tiles:
            return block(zz, 1 - y, c) * tiles + last
        return block(zz, y, c) * tiles + u

    def up_copy(zz, u):
        return copy(unit(zz, u), z_sem.at[zz * (tiles + 1) + u], up)

    def down_copy(zz, u):
        spot = jnp.where(zz == z, depth, zz)
        return copy(unit(zz, u), z_sem.at[spot * (tiles + 1) + u], down)

    def y_copy(zz, u):
        return copy(unit(zz, u), y_sem.at[zz * tiles + u], across)

    def c_copy(zz, yy, u):
        return copy(block(zz, yy, c) * tiles + u, c_sem.at[(zz * 2 + yy) * tiles + u], twin)

    barrier = pltpu.get_barrier_semaphore()
    pl.semaphore_signal(barrier, inc=1, device_id={"rep": across}, device_id_type=MESH)
    pl.semaphore_signal(barrier, inc=1, device_id={"rep": twin}, device_id_type=MESH)

    @pl.when(has_up)
    def _():
        pl.semaphore_signal(barrier, inc=1, device_id={"rep": up}, device_id_type=MESH)

    @pl.when(has_down)
    def _():
        pl.semaphore_signal(barrier, inc=1, device_id={"rep": down}, device_id_type=MESH)

    fetch = pltpu.make_async_copy(adj_ref, adj.at[pl.ds(0, stored)], adj_sem)
    fetch.start()
    projected = jnp.dot(
        feat_ref[...].astype(jnp.bfloat16), weight_ref[...], preferred_element_type=jnp.float32
    ).astype(jnp.bfloat16)
    for u in range(tiles):
        held[me * tiles + u] = projected[u * rows:(u + 1) * rows]
    adj[stored] = jnp.zeros((rows, rows), jnp.bfloat16)
    pl.semaphore_wait(barrier, 2 + has_up.astype(jnp.int32) + has_down.astype(jnp.int32))

    y_copy(z, last).start()
    for u in range(tiles):
        @pl.when(has_up)
        def _():
            up_copy(z, u).start()

        @pl.when(has_down)
        def _():
            down_copy(z, u).start()

        if u != last:
            y_copy(z, u).start()
    for u in range(tiles):
        c_copy(z, y, u).start()

    out_ref[...] = jnp.zeros_like(out_ref)

    def consume(b):
        for pair in range(tiles // 2):
            first = b * tiles + 2 * pair
            right = jnp.concatenate([held[first], held[first + 1]], axis=0)
            left = jnp.concatenate([
                jnp.concatenate([adj[slot_ref[r * every + first]],
                                 adj[slot_ref[r * every + first + 1]]], axis=1)
                for r in range(tiles)], axis=0)
            out_ref[...] += jnp.dot(left, right, preferred_element_type=jnp.float32)

    def take(zz, yy, flip):
        b = block(zz, yy, c + flip * (1 - 2 * c))

        @pl.when(flip == 1)
        def _():
            for u in range(tiles):
                arrived(b * tiles + u)

        consume(b)

    arrived(unit(z, tiles))

    @pl.when(has_up)
    def _():
        up_copy(z, tiles).start()

    @pl.when(has_down)
    def _():
        down_copy(z, tiles).start()

    c_copy(z, 1 - y, last).start()
    fetch.wait()

    @pl.loop(0, 2)
    def _(flip):
        take(z, y, flip)

    @pl.loop(1, depth + 1)
    def _(hop):
        for u in range(tiles + 1):
            for sign in (-1, 1):
                zz = z + sign * hop

                @pl.when((zz >= 0) & (zz < depth))
                def _():
                    arrived(unit(zz, u))
                    if sign == -1:
                        @pl.when(has_up)
                        def _():
                            up_copy(zz, u).start()
                    else:
                        @pl.when(has_down)
                        def _():
                            down_copy(zz, u).start()
                    if u < last:
                        y_copy(zz, u).start()
                    if u == tiles:
                        c_copy(zz, 1 - y, last).start()
                    else:
                        c_copy(zz, y, u).start()
            if u < last:
                for sign in (-1, 1):
                    zz = z + sign * (hop - 1)
                    fresh = (zz >= 0) & (zz < depth)
                    if sign == 1:
                        fresh = fresh & (hop > 1)

                    @pl.when(fresh)
                    def _():
                        arrived(block(zz, 1 - y, c) * tiles + u)
                        c_copy(zz, 1 - y, u).start()

        @pl.loop(0, 8)
        def _(i):
            flip = lax.rem(i, 2)
            side = lax.rem(i // 2, 2)
            older = i // 4
            distance = hop - older
            zz = z + distance * (2 * side - 1)
            yy = y + older * (1 - 2 * y)

            @pl.when((zz >= 0) & (zz < depth) & ((distance > 0) | (side == 0)))
            def _():
                take(zz, yy, flip)

    @pl.loop(0, depth)
    def _(zz):
        for u in range(tiles + 1):
            @pl.when(has_up & (zz <= z))
            def _():
                up_copy(zz, u).wait_send()

            @pl.when(has_down & (zz >= z))
            def _():
                down_copy(zz, u).wait_send()
        for u in range(tiles):
            if u < last:
                y_copy(zz, u).wait_send()
            c_copy(zz, 0, u).wait_send()
            c_copy(zz, 1, u).wait_send()
    y_copy(z, last).wait_send()


def shards(rep, features, weight, adjacency, col_tiles):
    tiles, stored, rows, _ = adjacency.shape
    width = features.shape[1]
    every = rep * tiles
    depth = rep // 4
    total = tiles * stored
    spots = jnp.arange(total, dtype=jnp.int32).reshape(tiles, stored)
    named = col_tiles[:, :, None] == jnp.arange(every, dtype=jnp.int32)
    slots = total + jnp.sum(jnp.where(named, spots[:, :, None] - total, 0), axis=1)
    summed = pl.pallas_call(
        functools.partial(kernel, depth, tiles),
        out_shape=jax.ShapeDtypeStruct(features.shape, jnp.float32),
        in_specs=[
            pl.BlockSpec(memory_space=pltpu.VMEM),
            pl.BlockSpec(memory_space=pltpu.VMEM),
            pl.BlockSpec(memory_space=pltpu.SMEM),
            pl.BlockSpec(memory_space=pl.ANY),
        ],
        out_specs=pl.BlockSpec(memory_space=pltpu.VMEM),
        scratch_shapes=[
            pltpu.VMEM((every, rows, width), jnp.bfloat16),
            pltpu.VMEM((total + 1, rows, rows), jnp.bfloat16),
            pltpu.SemaphoreType.DMA,
            pltpu.SemaphoreType.DMA((every,)),
            pltpu.SemaphoreType.DMA(((depth + 1) * (tiles + 1),)),
            pltpu.SemaphoreType.DMA((depth * tiles,)),
            pltpu.SemaphoreType.DMA((depth * 2 * tiles,)),
        ],
        compiler_params=pltpu.CompilerParams(
            collective_id=0, has_side_effects=True, vmem_limit_bytes=56 * 1024 * 1024),
        cost_estimate=pl.CostEstimate(
            flops=2 * tiles * every * rows * rows * width,
            bytes_accessed=total * rows * rows * 2, transcendentals=0),
    )(features, weight, slots.reshape(-1), adjacency.reshape(total, rows, rows))
    return jnp.maximum(summed, 0.0)


def solution(mesh):
    return jax.shard_map(
        functools.partial(shards, mesh.shape["rep"]),
        mesh=mesh,
        in_specs=(
            P(("groups", "rep"), None),
            P(),
            P(("groups", "rep"), None, None, None),
            P(("groups", "rep"), None),
        ),
        out_specs=P(("groups", "rep"), None),
        check_vma=False,
    )
```

time: 110 us -> 46.2 us (0.42)
  waiting for transfers between devices: 63.7 us -> 0 us
  Pallas kernels: 0 us -> 42.4 us
  matrix products: 17.2 us -> 0 us
  local copies, waits for them, and re-layouts: 14.8 us -> 0.67 us
  between operations: 13.4 us -> 0.02 us
  other arithmetic: 0.7 us -> 2.94 us
    all_gather x1 -> x0, waiting for transfers between devices: 63.7 us -> none  [shards(): everything = lax.all_gather(projected, 'rep', axis=0, tiled=True)]
    pallas_call x0 -> x1, Pallas kernels: none -> 42.4 us  [shards(): pl.pallas_call(functools.partial(kernel, depth, tiles), out_shape=jax.Sha...]
    dot_general x2 -> x0, matrix products: 17.2 us -> none  [the longest x1 15 us: shards(): jnp.einsum('jkab,jkbf->jaf', adjacency, picked, preferred_element_type=jn...]
    gather x1 -> x0, local copies, waits for them, and re-layouts: 13.8 us -> none  [shards(): picked = source[col_tiles]]
    max x0 -> x1, other arithmetic: none -> 2.06 us  [shards(): return jnp.maximum(summed, 0.0)]
  transfers between devices with their start and end apart: 1 -> 0, of which waited for: 1 -> 0; matrix products, arithmetic and copies ran while one was open for 1% -> 0% of each run, Pallas kernels for 0% -> 0%
where the time goes in v1:
time: 46.2 us; the launch traced here: 46 us
  Pallas kernels  42.4 us (92%)
  other arithmetic  2.94 us (6%)
  local copies, waits for them, and re-layouts  0.67 us (1%)
    pallas_call x1, Pallas kernels, shards(): pl.pallas_call(functools.partial(kernel, depth, tiles), out_shape=jax.Sha...  42.4 us
    max x1, other arithmetic, shards(): return jnp.maximum(summed, 0.0)  2.06 us

profile of v1, /device:TPU:1, one launch (start us, length us, event | category | flops | bytes accessed | tf_op | source)
XLA Modules:
  0.0 46.0 jit_solution(4722667376837209985)
XLA Ops:
  0.0 0.9 %select_reduce_fusion = s32[6,96]{1,0:T(8,128)S(1)} fusion(s32[6,60]{1,0:T(8,128)S(1)} %add_add_fusion, s32[6,60]{1,0:T(8,128)} %param.7), kind=kLoop, calls=%fused_computation.1 | loop fusion | flops 103104 | bytes 5184 | tf_op jit(solution)/shard_map/reduce_sum | solution.py:207
  0.9 0.7 %add.24.slot_ref = s32[576]{0:T(1024)} reshape(s32[6,96]{1,0:T(8,128)S(1)} %broadcast_add_fusion) | data formatting | bytes 4608 | tf_op jit(solution)/shard_map/add | solution.py:207
  1.6 42.4 %shard_map.46 = f32[768,256]{1,0:T(8,128)} custom-call(f32[768,256]{1,0:T(8,128)} %feat_ref.1, bf16[256,256]{1,0:T(8,128)(2,1)} %weight_ref.1, s32[576]{0:T(1024)} %add.24.slot_ref, bf16[360,128,128]{2,1,0:T(8,128)(2,1)} %bitcast.1), custom_call_target="tpu_custom_call" | custom-call | flops 4831838208 | bytes 11796480 | tf_op jit(solution)/shard_map/pallas_call | solution.py:208
  43.9 2.1 %broadcast_maximum_fusion = f32[768,256]{1,0:T(8,128)} fusion(f32[768,256]{1,0:T(8,128)} %shard_map.46), kind=kLoop, calls=%fused_computation | loop fusion | flops 196608 | bytes 1572864 | tf_op jit(solution)/shard_map/max | solution.py:233
  (2 shorter events, 0.0 us)

commit v2 on v1

--- a/solution.py
+++ b/solution.py
@@ -10,12 +10,14 @@
 MESH = pl.DeviceIdType.MESH
 
 
-def kernel(depth, tiles, feat_ref, weight_ref, slot_ref, adj_ref, out_ref,
-           held, adj, adj_sem, recv_sem, z_sem, y_sem, c_sem):
+def kernel(depth, tiles, feat_hbm, weight_hbm, cols_hbm, adj_hbm, out_ref,
+           held, adj, feat, weight, cols, table, slot_ref,
+           in_sem, recv_sem, z_sem, y_sem, c_sem):
     rep = depth * 4
     every = rep * tiles
     rows = held.shape[1]
-    stored = adj_ref.shape[0]
+    stored = cols_hbm.shape[1]
+    total = tiles * stored
     last = tiles - 1
     me = lax.axis_index("rep")
     c = lax.rem(me, 2)
@@ -66,18 +68,35 @@
     def _():
         pl.semaphore_signal(barrier, inc=1, device_id={"rep": down}, device_id_type=MESH)
 
-    fetch = pltpu.make_async_copy(adj_ref, adj.at[pl.ds(0, stored)], adj_sem)
-    fetch.start()
-    projected = jnp.dot(
-        feat_ref[...].astype(jnp.bfloat16), weight_ref[...], preferred_element_type=jnp.float32
-    ).astype(jnp.bfloat16)
-    for u in range(tiles):
-        held[me * tiles + u] = projected[u * rows:(u + 1) * rows]
-    adj[stored] = jnp.zeros((rows, rows), jnp.bfloat16)
+    def fetch(source, target, n):
+        return pltpu.make_async_copy(source, target, in_sem.at[n])
+
+    fetch_weight = fetch(weight_hbm, weight, 0)
+    fetch_cols = fetch(cols_hbm, cols, 1)
+    fetch_adj = fetch(adj_hbm, adj.at[pl.ds(0, total)], 2)
+    fetch_feat = [fetch(feat_hbm.at[pl.ds(u * rows, rows)], feat.at[pl.ds(u * rows, rows)], 3 + u)
+                  for u in range(tiles)]
+    fetch_weight.start()
+    order = [last] + list(range(last))
+    for u in order:
+        fetch_feat[u].start()
+    fetch_cols.start()
+    fetch_adj.start()
+
+    def project(u):
+        fetch_feat[u].wait()
+        held[me * tiles + u] = jnp.dot(
+            feat[u * rows:(u + 1) * rows].astype(jnp.bfloat16), weight[...],
+            preferred_element_type=jnp.float32).astype(jnp.bfloat16)
+
+    fetch_weight.wait()
+    project(last)
     pl.semaphore_wait(barrier, 2 + has_up.astype(jnp.int32) + has_down.astype(jnp.int32))
-
     y_copy(z, last).start()
     for u in range(tiles):
+        if u != last:
+            project(u)
+
         @pl.when(has_up)
         def _():
             up_copy(z, u).start()
@@ -88,9 +107,19 @@
 
         if u != last:
             y_copy(z, u).start()
-    for u in range(tiles):
         c_copy(z, y, u).start()
 
+    fetch_cols.wait()
+    named = cols[...]
+    lane = lax.broadcasted_iota(jnp.int32, (tiles, every), 1)
+    base = lax.broadcasted_iota(jnp.int32, (tiles, every), 0) * stored
+    slots = jnp.full((tiles, every), total, jnp.int32)
+    for k in range(stored):
+        slots = jnp.where(named[:, k:k + 1] == lane, base + k, slots)
+    table[...] = slots
+    publish = fetch(table, slot_ref, 1)
+    publish.start()
+    adj[total] = jnp.zeros((rows, rows), jnp.bfloat16)
     out_ref[...] = jnp.zeros_like(out_ref)
 
     def consume(b):
@@ -98,8 +127,8 @@
             first = b * tiles + 2 * pair
             right = jnp.concatenate([held[first], held[first + 1]], axis=0)
             left = jnp.concatenate([
-                jnp.concatenate([adj[slot_ref[r * every + first]],
-                                 adj[slot_ref[r * every + first + 1]]], axis=1)
+                jnp.concatenate([adj[slot_ref[r, first]],
+                                 adj[slot_ref[r, first + 1]]], axis=1)
                 for r in range(tiles)], axis=0)
             out_ref[...] += jnp.dot(left, right, preferred_element_type=jnp.float32)
 
@@ -124,7 +153,8 @@
         down_copy(z, tiles).start()
 
     c_copy(z, 1 - y, last).start()
-    fetch.wait()
+    publish.wait()
+    fetch_adj.wait()
 
     @pl.loop(0, 2)
     def _(flip):
@@ -202,34 +232,32 @@
     every = rep * tiles
     depth = rep // 4
     total = tiles * stored
-    spots = jnp.arange(total, dtype=jnp.int32).reshape(tiles, stored)
-    named = col_tiles[:, :, None] == jnp.arange(every, dtype=jnp.int32)
-    slots = total + jnp.sum(jnp.where(named, spots[:, :, None] - total, 0), axis=1)
     summed = pl.pallas_call(
         functools.partial(kernel, depth, tiles),
         out_shape=jax.ShapeDtypeStruct(features.shape, jnp.float32),
-        in_specs=[
-            pl.BlockSpec(memory_space=pltpu.VMEM),
-            pl.BlockSpec(memory_space=pltpu.VMEM),
-            pl.BlockSpec(memory_space=pltpu.SMEM),
-            pl.BlockSpec(memory_space=pl.ANY),
-        ],
+        in_specs=[pl.BlockSpec(memory_space=pl.ANY)] * 4,
         out_specs=pl.BlockSpec(memory_space=pltpu.VMEM),
         scratch_shapes=[
             pltpu.VMEM((every, rows, width), jnp.bfloat16),
             pltpu.VMEM((total + 1, rows, rows), jnp.bfloat16),
-            pltpu.SemaphoreType.DMA,
+            pltpu.VMEM(features.shape, jnp.float32),
+            pltpu.VMEM(weight.shape, jnp.bfloat16),
+            pltpu.VMEM(col_tiles.shape, jnp.int32),
+            pltpu.VMEM((tiles, every), jnp.int32),
+            pltpu.SMEM((tiles, every), jnp.int32),
+            pltpu.SemaphoreType.DMA((3 + tiles,)),
             pltpu.SemaphoreType.DMA((every,)),
             pltpu.SemaphoreType.DMA(((depth + 1) * (tiles + 1),)),
             pltpu.SemaphoreType.DMA((depth * tiles,)),
             pltpu.SemaphoreType.DMA((depth * 2 * tiles,)),
         ],
         compiler_params=pltpu.CompilerParams(
-            collective_id=0, has_side_effects=True, vmem_limit_bytes=56 * 1024 * 1024),
+            collective_id=0, has_side_effects=True,
+            vmem_limit_bytes=56 * 1024 * 1024),
         cost_estimate=pl.CostEstimate(
             flops=2 * tiles * every * rows * rows * width,
             bytes_accessed=total * rows * rows * 2, transcendentals=0),
-    )(features, weight, slots.reshape(-1), adjacency.reshape(total, rows, rows))
+    )(features, weight, col_tiles, adjacency.reshape(total, rows, rows))
     return jnp.maximum(summed, 0.0)
 
 

time: 46.2 us -> 43.7 us (0.946)
  Pallas kernels: 42.4 us -> 41.5 us
  other arithmetic: 2.94 us -> 2.06 us
  local copies, waits for them, and re-layouts: 0.67 us -> 0 us
    pallas_call x1, Pallas kernels: 42.4 us -> 41.5 us  [shards(): pl.pallas_call(functools.partial(kernel, depth, tiles), out_shape=jax.Sha...]
    reduce_sum x1 -> x0, other arithmetic: 0.86 us -> none  [shards(): jnp.sum(jnp.where(named, spots[:, :, None] - total, 0), axis=1)]
    add x1 -> x0, local copies, waits for them, and re-layouts: 0.67 us -> none  [shards(): total + jnp.sum(jnp.where(named, spots[:, :, None] - total, 0), axis=1)]
where the time goes in v2:
time: 43.7 us; the launch traced here: 43.5 us
  Pallas kernels  41.5 us (95%)
  other arithmetic  2.06 us (5%)
    pallas_call x1, Pallas kernels, shards(): pl.pallas_call(functools.partial(kernel, depth, tiles), out_shape=jax.Sha...  41.5 us
    max x1, other arithmetic, shards(): return jnp.maximum(summed, 0.0)  2.06 us

profile of v2, /device:TPU:1, one launch (start us, length us, event | category | flops | bytes accessed | tf_op | source)
XLA Modules:
  0.0 43.5 jit_solution(5210549299921261581)
XLA Ops:
  0.0 41.5 %shard_map.46 = f32[768,256]{1,0:T(8,128)} custom-call(f32[768,256]{1,0:T(8,128)} %feat_hbm.1, bf16[256,256]{1,0:T(8,128)(2,1)} %weight_hbm.1, s32[6,60]{1,0:T(8,128)} %cols_hbm.1, bf16[360,128,128]{2,1,0:T(8,128)(2,1)} %bitcast.1), custom_call_target="tpu_custom_call" | custom-call | flops 4831838208 | bytes 11796480 | tf_op jit(solution)/shard_map/pallas_call | solution.py:235
  41.5 2.1 %broadcast_maximum_fusion = f32[768,256]{1,0:T(8,128)} fusion(f32[768,256]{1,0:T(8,128)} %shard_map.46), kind=kLoop, calls=%fused_computation | loop fusion | flops 196608 | bytes 1572864 | tf_op jit(solution)/shard_map/max | solution.py:261

commit v3 on v2

--- a/solution.py
+++ b/solution.py
@@ -253,7 +253,7 @@
         ],
         compiler_params=pltpu.CompilerParams(
             collective_id=0, has_side_effects=True,
-            vmem_limit_bytes=56 * 1024 * 1024),
+            vmem_limit_bytes=53 * 1024 * 1024),
         cost_estimate=pl.CostEstimate(
             flops=2 * tiles * every * rows * rows * width,
             bytes_accessed=total * rows * rows * 2, transcendentals=0),

time: 43.7 us -> 43.3 us (level)
  local copies, waits for them, and re-layouts: 0 us -> 1.59 us
  other arithmetic: 2.06 us -> 0.93 us
  Pallas kernels: 41.5 us -> 40.6 us
    unnamed x0 -> x4, local copies, waits for them, and re-layouts: none -> 1.59 us
    max x1, other arithmetic: 2.06 us -> 0.93 us  [shards(): return jnp.maximum(summed, 0.0)]
    pallas_call x1, Pallas kernels: 41.5 us -> 40.6 us  [shards(): pl.pallas_call(functools.partial(kernel, depth, tiles), out_shape=jax.Sha...]
where the time goes in v3:
time: 43.3 us; the launch traced here: 43.1 us
  Pallas kernels  40.6 us (94%)
  local copies, waits for them, and re-layouts  1.59 us (4%)
  other arithmetic  0.93 us (2%)
    pallas_call x1, Pallas kernels, shards(): pl.pallas_call(functools.partial(kernel, depth, tiles), out_shape=jax.Sha...  40.6 us
    unnamed x4, local copies, waits for them, and re-layouts  1.59 us
    max x1, other arithmetic, shards(): return jnp.maximum(summed, 0.0)  0.93 us

profile of v3, /device:TPU:1, one launch (start us, length us, event | category | flops | bytes accessed | tf_op | source)
XLA Modules:
  0.0 43.1 jit_solution(11349408106143730699)
XLA Ops:
  0.0 0.0 copy-start
  0.0 0.9 %copy-done = bf16[256,256]{1,0:T(8,128)(2,1)S(1)} copy-done((bf16[256,256]{1,0:T(8,128)(2,1)S(1)}, bf16[256,256]{1,0:T(8,128)(2,1)}, u32[]{:S(2)}) %copy-start) | copy-done | bytes 131096
  0.9 0.0 copy-start.1
  0.9 0.7 %copy-done.1 = s32[6,60]{1,0:T(8,128)S(1)} copy-done((s32[6,60]{1,0:T(8,128)S(1)}, s32[6,60]{1,0:T(8,128)}, u32[]{:S(2)}) %copy-start.1) | copy-done | bytes 1464
  1.6 40.6 %shard_map.46 = f32[768,256]{1,0:T(8,128)S(1)} custom-call(f32[768,256]{1,0:T(8,128)} %feat_hbm.1, bf16[256,256]{1,0:T(8,128)(2,1)S(1)} %copy-done, s32[6,60]{1,0:T(8,128)S(1)} %copy-done.1, bf16[360,128,128]{2,1,0:T(8,128)(2,1)} %bitcast.1), custom_call_target="tpu_custom_call" | custom-call | flops 4831838208 | bytes 11796480 | tf_op jit(solution)/shard_map/pallas_call | solution.py:235
  42.2 0.9 %broadcast_maximum_fusion = f32[768,256]{1,0:T(8,128)} fusion(f32[768,256]{1,0:T(8,128)S(1)} %shard_map.46), kind=kLoop, calls=%fused_computation | loop fusion | flops 196608 | bytes 1572864 | tf_op jit(solution)/shard_map/max | solution.py:261
Async XLA Ops:
  0.0 0.9 %copy-start = (bf16[256,256]{1,0:T(8,128)(2,1)S(1)}, bf16[256,256]{1,0:T(8,128)(2,1)}, u32[]{:S(2)}) copy-start(bf16[256,256]{1,0:T(8,128)(2,1)} %weight_hbm.1) | copy-start | bytes 393220
  0.9 0.7 %copy-start.1 = (s32[6,60]{1,0:T(8,128)S(1)}, s32[6,60]{1,0:T(8,128)}, u32[]{:S(2)}) copy-start(s32[6,60]{1,0:T(8,128)} %cols_hbm.1) | copy-start | bytes 4324

commit v4 on v3

--- a/solution.py
+++ b/solution.py
@@ -123,14 +123,12 @@
     out_ref[...] = jnp.zeros_like(out_ref)
 
     def consume(b):
-        for pair in range(tiles // 2):
-            first = b * tiles + 2 * pair
-            right = jnp.concatenate([held[first], held[first + 1]], axis=0)
-            left = jnp.concatenate([
-                jnp.concatenate([adj[slot_ref[r, first]],
-                                 adj[slot_ref[r, first + 1]]], axis=1)
-                for r in range(tiles)], axis=0)
-            out_ref[...] += jnp.dot(left, right, preferred_element_type=jnp.float32)
+        first = b * tiles
+        right = held[pl.ds(first, tiles)].reshape(tiles * rows, -1)
+        left = jnp.concatenate([
+            jnp.concatenate([adj[slot_ref[r, first + u]] for u in range(tiles)], axis=1)
+            for r in range(tiles)], axis=0)
+        out_ref[...] += jnp.dot(left, right, preferred_element_type=jnp.float32)
 
     def take(zz, yy, flip):
         b = block(zz, yy, c + flip * (1 - 2 * c))

time: 43.3 us -> 43.3 us (level)
  no operation moved by 1% of the time
where the time goes in v4:
time: 43.3 us; the launch traced here: 43.2 us
  Pallas kernels  40.6 us (94%)
  local copies, waits for them, and re-layouts  1.59 us (4%)
  other arithmetic  0.93 us (2%)
    pallas_call x1, Pallas kernels, shards(): pl.pallas_call(functools.partial(kernel, depth, tiles), out_shape=jax.Sha...  40.6 us
    unnamed x4, local copies, waits for them, and re-layouts  1.59 us
    max x1, other arithmetic, shards(): return jnp.maximum(summed, 0.0)  0.93 us

profile of v4, /device:TPU:1, one launch (start us, length us, event | category | flops | bytes accessed | tf_op | source)
XLA Modules:
  0.0 43.2 jit_solution(8234269862642624992)
XLA Ops:
  0.0 0.0 copy-start
  0.0 0.9 %copy-done = bf16[256,256]{1,0:T(8,128)(2,1)S(1)} copy-done((bf16[256,256]{1,0:T(8,128)(2,1)S(1)}, bf16[256,256]{1,0:T(8,128)(2,1)}, u32[]{:S(2)}) %copy-start) | copy-done | bytes 131096
  0.9 0.0 copy-start.1
  0.9 0.7 %copy-done.1 = s32[6,60]{1,0:T(8,128)S(1)} copy-done((s32[6,60]{1,0:T(8,128)S(1)}, s32[6,60]{1,0:T(8,128)}, u32[]{:S(2)}) %copy-start.1) | copy-done | bytes 1464
  1.6 40.6 %shard_map.46 = f32[768,256]{1,0:T(8,128)S(1)} custom-call(f32[768,256]{1,0:T(8,128)} %feat_hbm.1, bf16[256,256]{1,0:T(8,128)(2,1)S(1)} %copy-done, s32[6,60]{1,0:T(8,128)S(1)} %copy-done.1, bf16[360,128,128]{2,1,0:T(8,128)(2,1)} %bitcast.1), custom_call_target="tpu_custom_call" | custom-call | flops 4831838208 | bytes 11796480 | tf_op jit(solution)/shard_map/pallas_call | solution.py:233
  42.2 0.9 %broadcast_maximum_fusion = f32[768,256]{1,0:T(8,128)} fusion(f32[768,256]{1,0:T(8,128)S(1)} %shard_map.46), kind=kLoop, calls=%fused_computation | loop fusion | flops 196608 | bytes 1572864 | tf_op jit(solution)/shard_map/max | solution.py:259
Async XLA Ops:
  0.0 0.9 %copy-start = (bf16[256,256]{1,0:T(8,128)(2,1)S(1)}, bf16[256,256]{1,0:T(8,128)(2,1)}, u32[]{:S(2)}) copy-start(bf16[256,256]{1,0:T(8,128)(2,1)} %weight_hbm.1) | copy-start | bytes 393220
  0.9 0.7 %copy-start.1 = (s32[6,60]{1,0:T(8,128)S(1)}, s32[6,60]{1,0:T(8,128)}, u32[]{:S(2)}) copy-start(s32[6,60]{1,0:T(8,128)} %cols_hbm.1) | copy-start | bytes 4324
